TPU v7x, 256 devices: a whole 4x4x8 slice. The times are simulated.
256 devices in a mesh: row: 8 (over z_lo, core), col: 32 (over z_hi, y, x).
Axes of the slice: x: 4, y: 4, z: 8 (z_hi: 2, z_lo: 4; z = z_hi * 4 + z_lo), core: 2. Of those that a mesh axis runs over, the one named last changes fastest.
Arguments:
- right_env: bfloat16 [8, 8, 9, 262144], P('row', None, None, 'col'), may hold values from -45 to 45
- left_env: bfloat16 [8, 8, 9, 262144], P('row', None, None, 'col'), may hold values from -45 to 45
- down_env: bfloat16 [8, 8, 9, 262144], P('row', None, None, 'col'), may hold values from -45 to 45
- up_env: bfloat16 [8, 8, 9, 262144], P('row', None, None, 'col'), may hold values from -45 to 45
- hamiltonian: float32 [9, 9], replicated, may hold values from -0.625 to 0.625
- parity: int32 [8], replicated, may hold values 0 or 1
Outputs:
- grad_right: bfloat16 [8, 8, 9, 262144], P('row', None, None, 'col')
- grad_left: bfloat16 [8, 8, 9, 262144], P('row', None, None, 'col')
- grad_down: bfloat16 [8, 8, 9, 262144], P('row', None, None, 'col')
- grad_up: bfloat16 [8, 8, 9, 262144], P('row', None, None, 'col')
- energy: float32 [], replicated
All inputs are finite; a program needn't handle non-finite values.
Results may differ from a plain program's by a relative error of at most 0.0051.
Values may be sent and summed in bfloat16 or wider, within the bound.
A program may use at most 128 MiB of HBM per device.

v0:
```python
import jax
import jax.numpy as jnp
from jax import lax
from jax.sharding import PartitionSpec as P


def shifted(value, axis, steps):
    count = lax.axis_size(axis)
    initial, last = (max(0, -steps), min(count, count - steps))
    return lax.ppermute(value, axis, [(source, source + steps) for source in range(initial, last)])


def phys_parity():
    return jnp.minimum(jnp.arange(3, dtype=jnp.int32), 1)


def pair_signs(parity, leg_count):
    bond_dim = parity.shape[0]
    charge = phys_parity()
    exponent = (
        charge[:, None, None, None] * parity[None, None, :, None]
        + charge[None, :, None, None] * parity[None, None, None, :]
    )
    swap_sign = (1 - 2 * (exponent % 2)).astype(jnp.float32).reshape(9, 1, bond_dim * bond_dim)
    return jnp.broadcast_to(swap_sign, (9, leg_count, bond_dim * bond_dim)).reshape(
        9, leg_count * bond_dim * bond_dim
    )


def charge_mask():
    charge = phys_parity()
    ket_charge = charge[:, None, None, None] + charge[None, None, :, None]
    bra_charge = charge[None, :, None, None] + charge[None, None, None, :]
    return (ket_charge == bra_charge).astype(jnp.float32).reshape(9, 9)


def partial_density(first_env, second, swap_sign):
    signed = second * swap_sign.astype(jnp.bfloat16)
    density = jnp.einsum("rcpm,rcqm->rcpq", first_env, signed, preferred_element_type=jnp.float32)
    return (density, signed)


def bond_finish(density, coupling, weight, valid_mask):
    frob_norm = jnp.sqrt(jnp.mean(density * density, axis=(2, 3)) + 1e-06)
    trace_val = jnp.sum(coupling * density, axis=(2, 3))
    factor = valid_mask * weight
    energy = factor * trace_val / frob_norm
    entries = density.shape[2] * density.shape[3]
    bond_lam = factor[:, :, None, None] * (
        coupling / frob_norm[:, :, None, None]
        - (trace_val / (entries * frob_norm**3))[:, :, None, None] * density
    )
    return (energy, bond_lam.astype(jnp.bfloat16))


def bond_grads(bond_lam, first_env, signed, swap_sign):
    grad_first = jnp.einsum("rcpq,rcqm->rcpm", bond_lam, signed, preferred_element_type=jnp.float32)
    grad_second = swap_sign * jnp.einsum(
        "rcpq,rcpm->rcqm", bond_lam, first_env, preferred_element_type=jnp.float32
    )
    return (grad_first, grad_second)


def ramp_weight(row_pos, col_pos, row_total, col_total):
    return 1.0 + 2.0 * col_pos / col_total + row_pos / row_total


def square_sum(pieces):
    total = jnp.zeros((), jnp.float32)
    for piece in pieces:
        total = total + jnp.sum(piece * piece)
    return total


def shards(right_env, left_env, down_env, up_env, hamiltonian, parity):
    row_count = right_env.shape[0]
    col_total = right_env.shape[1]
    pair_count = right_env.shape[2]
    cut_local = right_env.shape[3]
    bond_dim = parity.shape[0]
    swap_sign = pair_signs(parity, cut_local // (bond_dim * bond_dim))
    coupling = hamiltonian * charge_mask()
    row_total = row_count * lax.axis_size("row")
    cut_total = cut_local * lax.axis_size("col")
    first_col = (lax.axis_index("col") == 0).astype(jnp.float32)
    row_glob = (lax.axis_index("row") * row_count + jnp.arange(row_count, dtype=jnp.int32)).astype(
        jnp.float32
    )
    col_glob = jnp.arange(col_total, dtype=jnp.int32).astype(jnp.float32)
    zero_column = jnp.zeros((row_count, 1, pair_count, cut_local), right_env.dtype)
    zero_grad = jnp.zeros((row_count, 1, pair_count, cut_local), jnp.float32)
    seconds_h = jnp.concatenate([left_env[:, 1:], zero_column], axis=1)
    weight_h = ramp_weight(row_glob[:, None], col_glob[None, :], row_total, col_total)
    valid_h = (col_glob < col_total - 1).astype(jnp.float32)[None, :]
    dens_h, signed_h = partial_density(right_env, seconds_h, swap_sign)
    from_below = shifted(up_env, "row", -1)
    partner_v = jnp.concatenate([up_env[1:], from_below], axis=0)
    dens_v, signed_v = partial_density(down_env, partner_v, swap_sign)
    dens_h, dens_v = lax.psum((dens_h, dens_v), "col")
    valid_v = jnp.broadcast_to(
        (row_glob < row_total - 1).astype(jnp.float32)[:, None], (row_count, col_total)
    )
    energy_h, lam_h = bond_finish(dens_h, coupling, weight_h, valid_h)
    energy_v, lam_v = bond_finish(dens_v, coupling, weight_h, valid_v)
    grad_right, partner_h = bond_grads(lam_h, right_env, signed_h, swap_sign)
    grad_left = jnp.concatenate([zero_grad, partner_h[:, : col_total - 1]], axis=1)
    grad_down, grad_partner_v = bond_grads(lam_v, down_env, signed_v, swap_sign)
    energy_local = first_col * (jnp.sum(energy_h) + jnp.sum(energy_v))
    returned_v = shifted(grad_partner_v, "row", 1)
    grad_up = jnp.concatenate([returned_v, grad_partner_v[: row_count - 1]], axis=0)
    energy_total, square_total = lax.psum(
        (energy_local, square_sum((grad_right, grad_left, grad_down, grad_up))), ("row", "col")
    )
    count = 4.0 * row_total * col_total * pair_count * cut_total
    grad_scale = 1.0 / jnp.sqrt(square_total / count + 1e-06)
    outputs = tuple(
        (
            (piece * grad_scale).astype(jnp.bfloat16)
            for piece in (grad_right, grad_left, grad_down, grad_up)
        )
    )
    return (outputs[0], outputs[1], outputs[2], outputs[3], energy_total / col_total)


def solution(mesh):
    in_specs = (
        P("row", None, None, "col"),
        P("row", None, None, "col"),
        P("row", None, None, "col"),
        P("row", None, None, "col"),
        P(),
        P(),
    )
    out_specs = (
        P("row", None, None, "col"),
        P("row", None, None, "col"),
        P("row", None, None, "col"),
        P("row", None, None, "col"),
        P(),
    )
    return jax.shard_map(shards, mesh=mesh, in_specs=in_specs, out_specs=out_specs, check_vma=False)
```

profile of v0, /device:TPU:1, one launch (start us, length us, event | category | flops | bytes accessed | tf_op | source)
XLA Modules:
  0.0 372.4 jit_solution(15733434108351140243)
XLA Ops:
  0.6 5.3 %collective-permute-start = (bf16[1,8,9,8192]{3,1,2,0:T(8,128)(2,1)}, bf16[1,8,9,8192]{3,1,2,0:T(8,128)(2,1)}, u32[]{:S(2)}, u32[]{:S(2)}) collective-permute-start(bf16[1,8,9,8192]{3,1,2,0:T(8,128)(2,1)} %param.9), channel_id=1, source_target_pairs={{32,0},{64,32},{96,64},{128,96},{160,128},{192,160},{224,192},{33,... | collective-permute-start | bytes 3538952 | tf_op jit(solution)/shard_map/ppermute | solution.py:10
  5.9 0.7 broadcast_multiply_fusion
  6.9 0.2 reshape.371
  7.2 1.7 slice.6
  9.1 0.1 copy.41
  9.2 10.7 %collective-permute-done = bf16[1,8,9,8192]{3,1,2,0:T(8,128)(2,1)} collective-permute-done((bf16[1,8,9,8192]{3,1,2,0:T(8,128)(2,1)}, bf16[1,8,9,8192]{3,1,2,0:T(8,128)(2,1)}, u32[]{:S(2)}, u32[]{:S(2)}) %collective-permute-start) | collective-permute-done | bytes 1179680 | tf_op jit(solution)/shard_map/ppermute | solution.py:10
  19.9 1.8 multiply_bitcast_fusion
  21.8 1.3 fusion.19
  23.2 1.5 fusion.24
  24.6 198.1 %all-reduce.3 = (f32[1,8,9,9]{2,3,1,0:T(8,128)S(1)}, f32[1,8,9,9]{2,3,1,0:T(8,128)S(1)}) all-reduce(f32[1,8,9,9]{2,3,1,0:T(8,128)S(1)} %fusion.19, f32[1,8,9,9]{2,3,1,0:T(8,128)S(1)} %fusion.24), channel_id=1, replica_groups=mesh['row'=8,'col'=32] {'col'}, use_global_device_ids=true, to_apply=%region_0.1 | all-reduce | flops 1296 | bytes 10368 | tf_op jit(solution)/shard_map/psum | solution.py:99
  222.7 0.2 multiply_reduce_fusion.4
  222.8 1.3 multiply_reduce_fusion.7
  224.1 1.6 fusion
  225.7 2.8 copy.52
  228.6 29.9 %collective-permute-start.1 = (f32[1,8,9,8192]{3,1,2,0:T(8,128)}, f32[1,8,9,8192]{3,1,2,0:T(8,128)S(1)}, u32[]{:S(2)}, u32[]{:S(2)}) collective-permute-start(f32[1,8,9,8192]{3,1,2,0:T(8,128)} %copy.52), channel_id=1, source_target_pairs={{0,32},{32,64},{64,96},{96,128},{128,160},{160,192},{192,224},{1,3... | collective-permute-start | bytes 7077896 | tf_op jit(solution)/shard_map/ppermute | solution.py:10
  258.5 3.0 fusion.1
  261.5 0.3 slice.8
  261.9 1.5 fusion.2
  263.4 0.6 copy-done.6
  264.0 4.2 %multiply_reduce_fusion.1 = (f32[]{:T(128)}, f32[8,9,8192]{2,1,0:T(8,128)}) fusion(bf16[8,9,8192]{2,0,1:T(8,128)(2,1)S(1)} %copy-done.6, f32[1,8,9,9]{2,3,1,0:T(8,128)S(1)} %copy-done.11, f32[8]{0:T(128)S(1)} %copy-done.15, f32[8]{0:T(128)S(1)} %copy-done.14, f32[9,9]{0,1:T(8,128)S(1)} %copy.41, f32[8]{0:T(128)S(1)} %compare_select_fusion), kind=kOutput, calls=%fused_computation.13 | convolution fusion | flops 11799719 | bytes 3541960 | tf_op jit(solution)/shard_map/rcpq,rcqm->rcpm/dot_general | solution.py:57
  269.5 5.6 %multiply_reduce_fusion = (f32[]{:T(128)}, f32[8,9,8192]{2,1,0:T(8,128)}) fusion(bf16[8,9,8192]{2,0,1:T(8,128)(2,1)} %copy-done.4, f32[1,8,9,9]{2,3,1,0:T(8,128)} %copy-done.9, f32[8]{0:T(128)S(1)} %get-tuple-element.36, f32[8]{0:T(128)} %copy-done.13, f32[9,9]{0,1:T(8,128)S(1)} %copy.41, f32[8]{0:T(128)S(1)} %get-tuple-element.29), kind=kOutput, calls=%fused_computation.12 | convolution fusion | flops 11799719 | bytes 3541960 | tf_op jit(solution)/shard_map/rcpq,rcqm->rcpm/dot_general | solution.py:57
  277.0 7.4 %collective-permute-done.1 = f32[1,8,9,8192]{3,1,2,0:T(8,128)S(1)} collective-permute-done((f32[1,8,9,8192]{3,1,2,0:T(8,128)}, f32[1,8,9,8192]{3,1,2,0:T(8,128)S(1)}, u32[]{:S(2)}, u32[]{:S(2)}) %collective-permute-start.1) | collective-permute-done | bytes 2359328 | tf_op jit(solution)/shard_map/ppermute | solution.py:10
  284.4 1.2 multiply_reduce_fusion.2
  286.2 72.4 %all-reduce.2 = (f32[]{:T(128)}, f32[]{:T(128)}) all-reduce(f32[]{:T(128)S(6)} %add.172, f32[]{:T(128)S(6)} %mul.264), channel_id=1, replica_groups=mesh['row'=8,'col'=32] {'row','col'}, use_global_device_ids=true, to_apply=%region_10.11 | all-reduce | flops 2 | bytes 16 | tf_op jit(solution)/shard_map/psum | solution.py:111
  359.3 2.3 fusion.3
  361.7 1.3 fusion.4
  363.0 1.7 copy.57
  364.8 0.3 fusion.18
  365.1 1.7 copy.56
  366.8 1.7 copy.55
  368.5 0.3 fusion.17
  368.8 1.7 copy.54
  (42 shorter events, 0.6 us)
Async XLA Ops:
  0.6 22.5 %copy-start = (bf16[1,8,9,8192]{3,1,2,0:T(8,128)(2,1)S(1)}, bf16[1,8,9,8192]{3,1,2,0:T(8,128)(2,1)}, u32[]{:S(2)}) copy-start(bf16[1,8,9,8192]{3,1,2,0:T(8,128)(2,1)} %param.8) | copy-start | bytes 3538948
  0.6 19.3 %collective-permute-start = (bf16[1,8,9,8192]{3,1,2,0:T(8,128)(2,1)}, bf16[1,8,9,8192]{3,1,2,0:T(8,128)(2,1)}, u32[]{:S(2)}, u32[]{:S(2)}) collective-permute-start(bf16[1,8,9,8192]{3,1,2,0:T(8,128)(2,1)} %param.9), channel_id=1, source_target_pairs={{32,0},{64,32},{96,64},{128,96},{160,128},{192,160},{224,192},{33,... | collective-permute-start | bytes 3538952 | tf_op jit(solution)/shard_map/ppermute | solution.py:10
  6.9 2.2 copy-start.12
  7.1 217.0 %copy-start.7 = (f32[9,8192]{1,0:T(8,128)}, f32[9,8192]{1,0:T(8,128)S(1)}, u32[]{:S(2)}) copy-start(f32[9,8192]{1,0:T(8,128)S(1)} %reshape.371) | copy-start | bytes 884740
  9.2 12.6 %copy-start.8 = (bf16[1,8,9,8192]{3,1,2,0:T(8,128)(2,1)S(1)}, bf16[1,8,9,8192]{3,1,2,0:T(8,128)(2,1)}, u32[]{:S(2)}) copy-start(bf16[1,8,9,8192]{3,1,2,0:T(8,128)(2,1)} %param.6) | copy-start | bytes 3538948
  21.8 1.4 copy-start.5
  21.8 1.4 copy-start.4
  222.7 3.0 copy-start.9
  222.7 3.0 copy-start.10
  224.1 1.6 copy-start.13
  228.6 55.8 %collective-permute-start.1 = (f32[1,8,9,8192]{3,1,2,0:T(8,128)}, f32[1,8,9,8192]{3,1,2,0:T(8,128)S(1)}, u32[]{:S(2)}, u32[]{:S(2)}) collective-permute-start(f32[1,8,9,8192]{3,1,2,0:T(8,128)} %copy.52), channel_id=1, source_target_pairs={{0,32},{32,64},{64,96},{96,128},{128,160},{160,192},{192,224},{1,3... | collective-permute-start | bytes 7077896 | tf_op jit(solution)/shard_map/ppermute | solution.py:10
  261.8 6.4 %copy-start.1 = (f32[1,7,9,8192]{3,2,1,0:T(8,128)}, f32[1,7,9,8192]{3,2,1,0:T(8,128)S(1)}, u32[]{:S(2)}) copy-start(f32[1,7,9,8192]{3,2,1,0:T(8,128)S(1)} %slice.8) | copy-start | bytes 6193156
  261.8 2.2 copy-start.6
  261.8 2.1 copy-start.11
  261.8 2.1 copy-start.14
  261.9 2.1 copy-start.15
  361.7 3.1 copy-start.3
  365.1 3.5 copy-start.2
where the time goes:
time: 373 us; the launch traced here: 372 us
  blocking collectives  270 us (72%)
  starting transfers between devices  35.2 us (9%)
  waiting for transfers between devices  18.1 us (5%)
  matrix products  17.2 us (5%)
  local copies, waits for them, and re-layouts  12.9 us (3%)
  other arithmetic  11.3 us (3%)
  between operations  7.28 us (2%)
    psum x1, blocking collectives, shards(): dens_h, dens_v = lax.psum((dens_h, dens_v), 'col')  198 us
    psum x1, blocking collectives, shards(): lax.psum((energy_local, square_sum((grad_right, grad_left, grad_down, gra...  72.4 us
    ppermute x2, starting transfers between devices, shifted(): lax.ppermute(value, axis, [(source, source + steps) for source in range(i...  35.2 us
    ppermute x2, waiting for transfers between devices, shifted(): lax.ppermute(value, axis, [(source, source + steps) for source in range(i...  18.1 us
    dot_general x2, matrix products, bond_grads(): jnp.einsum('rcpq,rcqm->rcpm', bond_lam, signed, preferred_element_type=jn...  9.8 us
    unnamed x36, local copies, waits for them, and re-layouts  7.6 us
  transfers between devices with their start and end apart: 2, of which 2 were waited for; matrix products, arithmetic and copies ran while one was open for 5% of the time, Pallas kernels for 0%

commit v1 on v0

v1 whole, which is shorter than its diff:
```python
import functools

import jax
import jax.numpy as jnp
from jax import lax
from jax.experimental import pallas as pl
from jax.experimental.pallas import tpu as pltpu
from jax.sharding import PartitionSpec as P

PAIRS = 9
SITES = 8
FLAT = PAIRS * SITES
BOND = 8
KINDS = 3 * PAIRS
LANES = 256
STEP = 1024
MESH = pl.DeviceIdType.MESH
HIGHEST = lax.Precision.HIGHEST
F32 = jnp.float32
BF16 = jnp.bfloat16


def iota(shape, dim):
    return lax.broadcasted_iota(jnp.int32, shape, dim)


def dot32(a, b):
    return jnp.dot(a, b, precision=HIGHEST, preferred_element_type=F32)


def dot16(a, b):
    return jnp.dot(a, b, preferred_element_type=F32)


def sign_tile(par):
    shape = (FLAT, 128)
    pair = iota(shape, 0) // SITES
    lane = iota(shape, 1) % (BOND * BOND)
    ket, bra = lane // BOND, lane % BOND
    par_ket = jnp.zeros(shape, jnp.int32)
    par_bra = jnp.zeros(shape, jnp.int32)
    for bond in range(BOND):
        value = par[bond]
        par_ket = jnp.where(ket == bond, value, par_ket)
        par_bra = jnp.where(bra == bond, value, par_bra)
    exponent = jnp.minimum(pair // 3, 1) * par_ket + jnp.minimum(pair % 3, 1) * par_bra
    return (1 - 2 * (exponent % 2)).astype(F32)


def compact(gram, shift):
    both = (FLAT, 2 * FLAT)
    row_site, col = iota(both, 0) % SITES, iota(both, 1)
    want = jnp.where(col < FLAT, row_site, row_site + shift)
    upper = jnp.where(col % SITES == want, gram[:FLAT, :], 0.0)
    spread = (2 * FLAT, LANES)
    source, lane = iota(spread, 0), iota(spread, 1)
    target = jnp.where(source < FLAT, PAIRS, 0) + (source % FLAT) // SITES
    upper = dot32(upper, (lane % KINDS == target).astype(F32))
    one = (FLAT, FLAT)
    lower = jnp.where(iota(one, 0) % SITES == iota(one, 1) % SITES, gram[FLAT:, FLAT:], 0.0)
    spread = (FLAT, LANES)
    source, lane = iota(spread, 0), iota(spread, 1)
    lower = dot32(lower, (lane % KINDS == 2 * PAIRS + source // SITES).astype(F32))
    keep = lane // KINDS == source // SITES
    upper = jnp.where(keep, upper, 0.0).reshape(PAIRS, SITES, LANES).sum(axis=0)
    lower = jnp.where(keep, lower, 0.0).reshape(PAIRS, SITES, LANES).sum(axis=0)
    if shift:
        lower = jnp.concatenate([lower[shift:], lower[:shift]], axis=0)
    return upper + lower


def lane_coupling(ham):
    shape = (PAIRS, PAIRS)
    p, q = iota(shape, 0), iota(shape, 1)

    def charge(state):
        return jnp.minimum(state, 1)

    same = charge(p // 3) + charge(q // 3) == charge(p % 3) + charge(q % 3)
    coupling = jnp.where(same, ham, 0.0)
    shape = (PAIRS, LANES)
    row, lane = iota(shape, 0), iota(shape, 1)
    wide = dot32(coupling, (lane % KINDS == row).astype(F32))
    return jnp.where(lane // KINDS == row, wide, 0.0).sum(axis=0, keepdims=True)


def finish(sums, coupling, factor):
    lane = iota((SITES, LANES), 1)
    density = jnp.where((lane % KINDS < PAIRS) & (lane < PAIRS * KINDS), sums, 0.0)
    entries = PAIRS * PAIRS
    norm = jnp.sqrt((density * density).sum(axis=1, keepdims=True) / entries + 1e-06)
    trace = (coupling * density).sum(axis=1, keepdims=True)
    energy = factor * trace / norm
    lam = factor * (coupling / norm - trace / (entries * norm**3) * density)
    return energy, lam.astype(BF16)


def block(rows, kind, shift, exact):
    shape = (FLAT, LANES)
    row, lane = iota(shape, 0), iota(shape, 1)
    tall = jnp.concatenate([rows] * PAIRS, axis=0)
    tall = jnp.where(lane // KINDS == row // SITES, tall, 0.0)
    shape = (LANES, FLAT)
    source, col = iota(shape, 0), iota(shape, 1)
    pick = (source % KINDS == kind * PAIRS + col // SITES).astype(F32)
    wide = dot32(tall, pick) if exact else dot16(tall.astype(BF16), pick.astype(BF16))
    shape = (FLAT, FLAT)
    return jnp.where(iota(shape, 1) % SITES == iota(shape, 0) % SITES + shift, wide, 0.0)


def block_t(rows, shift):
    if shift:
        rows = jnp.concatenate([rows[SITES - shift :], rows[: SITES - shift]], axis=0)
    shape = (FLAT, LANES)
    row, lane = iota(shape, 0), iota(shape, 1)
    tall = jnp.concatenate([rows] * PAIRS, axis=0)
    tall = jnp.where(lane % KINDS == row // SITES, tall, 0.0)
    shape = (LANES, FLAT)
    source, col = iota(shape, 0), iota(shape, 1)
    pick = source // KINDS == col // SITES
    wide = dot16(tall.astype(BF16), pick.astype(BF16))
    shape = (FLAT, FLAT)
    return jnp.where(iota(shape, 0) % SITES == iota(shape, 1) % SITES + shift, wide, 0.0)


def squares(sums, lam):
    weights = block(lam, 0, 0, False)
    first = block(sums, 1, 0, True)
    second = block(sums, 2, 0, True)
    total = dot32(weights, second) + dot32(first, weights)
    return (total * weights).sum()


def kernel(
    nx, ny, rows_total, cols_total,
    right, left, down, up, ham_hbm, par_hbm,
    g_right, g_left, g_down, g_up, energy,
    v_right, v_left, v_down, v_up, from_above, from_below, ham, par, sign,
    gram_h, gram_d, gram_u, buf_x, buf_y, buf_z, buf_above, buf_below, buf_row,
    load_sem, down_send, down_recv, up_send, up_recv,
    x_send, x_recv, y_send, y_recv, z_send, z_recv,
    above_send, above_recv, below_send, below_recv, row_send, row_recv,
):
    cut = right.shape[2]
    half = cut // 2
    steps = half // STEP
    row, col = lax.axis_index("row"), lax.axis_index("col")
    x, y, hi = col % nx, col // nx % ny, col // (nx * ny)
    plane = nx * ny
    has_above, has_below = row > 0, row < rows_total - 1

    pairs = (
        (ham_hbm, ham), (par_hbm, par), (right, v_right), (left, v_left), (down, v_down), (up, v_up),
    )
    loads = [
        pltpu.make_async_copy(source, target, load_sem.at[i]) for i, (source, target) in enumerate(pairs)
    ]
    for load in loads:
        load.start()

    same_x = [(row, hi * plane + y * nx + (x + i) % nx) for i in range(1, nx)]
    same_y = [(row, hi * plane + (y + i) % ny * nx + x) for i in range(1, ny)]
    partner = (row, (1 - hi) * plane + y * nx + x)
    mates = [((row + i) % rows_total, col) for i in range(1, rows_total)]
    here = y * nx + x
    aboves = [(row - 1, z * plane + here) for z in (0, 1)]
    belows = [(row + 1, z * plane + here) for z in (0, 1)]

    barrier = pltpu.get_barrier_semaphore()
    for device in same_x + same_y + [partner] + mates:
        pl.semaphore_signal(barrier, inc=1, device_id=device, device_id_type=MESH)

    @pl.when(has_above)
    def _():
        pl.semaphore_signal(barrier, inc=1, device_id=(row - 1, partner[1]), device_id_type=MESH)

    @pl.when(has_below)
    def _():
        pl.semaphore_signal(barrier, inc=1, device_id=(row + 1, partner[1]), device_id_type=MESH)

    count = len(same_x) + len(same_y) + 1 + len(mates)
    pl.semaphore_wait(barrier, count + has_above.astype(jnp.int32) + has_below.astype(jnp.int32))

    def span(start):
        return pl.ds(pl.multiple_of(start, STEP), STEP)

    def send_down(i):
        at = span(i * STEP)
        return pltpu.make_async_remote_copy(
            down.at[:, :, at], from_above.at[:, :, at], down_send.at[i], down_recv.at[i],
            device_id=(row + 1, col), device_id_type=MESH,
        )

    def up_start(i):
        return (i * STEP + half) % cut

    def send_up(i):
        at = span(up_start(i))
        return pltpu.make_async_remote_copy(
            up.at[:, :, at], from_below.at[:, :, at], up_send.at[i], up_recv.at[i],
            device_id=(row - 1, col), device_id_type=MESH,
        )

    def start_bulk(i):
        @pl.when(has_below)
        def _():
            send_down(i).start()

        @pl.when(has_above)
        def _():
            send_up(i).start()

    for i in range(steps):
        start_bulk(i)

    for load in loads[:2]:
        load.wait()
    tile = sign_tile(par)
    sign[...] = jnp.concatenate([tile] * (STEP // 128), axis=1)
    coupling = lane_coupling(ham[...])

    def flat(ref, at):
        return ref[:, :, at].reshape(FLAT, STEP)

    def signed(ref, at):
        return (flat(ref, at).astype(F32) * sign[...]).astype(BF16)

    def add_gram(gram, first, second):
        data = jnp.concatenate([first, second], axis=0)
        gram[...] += lax.dot_general(data, data, (((1,), (1,)), ((), ())), preferred_element_type=F32)

    for gram in (gram_h, gram_d, gram_u):
        gram[...] = jnp.zeros_like(gram)
    for load in loads[2:]:
        load.wait()

    @pl.loop(0, 2 * steps)
    def _(i):
        at = span(i * STEP)
        add_gram(gram_h, flat(v_right, at), signed(v_left, at))

    @pl.loop(0, steps)
    def _(i):
        at = span(i * STEP)

        @pl.when(has_above)
        def _():
            send_down(i).wait_recv()
            add_gram(gram_u, flat(from_above, at), signed(v_up, at))

        at_up = span(up_start(i))

        @pl.when(has_below)
        def _():
            send_up(i).wait_recv()
            add_gram(gram_d, flat(v_down, at_up), signed(from_below, at_up))
            send_down(i).wait_send()
            send_down(i + steps).start()

        @pl.when(has_above)
        def _():
            send_up(i).wait_send()
            send_up(i + steps).start()

    sums = jnp.concatenate(
        [compact(gram_h[...], 1), compact(gram_d[...], 0), compact(gram_u[...], 0)], axis=1
    )

    def gather(value, buf, me, devices, send, recv):
        buf[me] = value
        copies = [
            pltpu.make_async_remote_copy(
                buf.at[me], buf.at[me], send.at[i], recv.at[me], device_id=device, device_id_type=MESH
            )
            for i, device in enumerate(devices)
        ]
        for copy in copies:
            copy.start()
        return copies

    def arrived(buf, slot, recv):
        pltpu.make_async_remote_copy(
            buf.at[slot], buf.at[slot], recv.at[slot], recv.at[slot], device_id=(row, col), device_id_type=MESH
        ).wait_recv()

    def total(buf):
        value = buf[0]
        for i in range(1, buf.shape[0]):
            value = value + buf[i]
        return value

    sends = gather(sums, buf_x, x, same_x, x_send, x_recv)
    for i in range(1, nx):
        arrived(buf_x, (x + i) % nx, x_recv)
    sums = total(buf_x)
    sends += gather(sums, buf_y, y, same_y, y_send, y_recv)
    for i in range(1, ny):
        arrived(buf_y, (y + i) % ny, y_recv)
    sums = total(buf_y)

    sends += gather(sums, buf_z, hi, [partner], z_send, z_recv)

    def to_below(z):
        return pltpu.make_async_remote_copy(
            buf_z.at[hi, :, pl.ds(LANES, LANES)], buf_above.at[hi],
            below_send.at[z], above_recv.at[hi], device_id=belows[z], device_id_type=MESH,
        )

    def to_above(z):
        return pltpu.make_async_remote_copy(
            buf_z.at[hi, :, pl.ds(2 * LANES, LANES)], buf_below.at[hi],
            above_send.at[z], below_recv.at[hi], device_id=aboves[z], device_id_type=MESH,
        )

    @pl.when(has_below)
    def _():
        for z in (0, 1):
            to_below(z).start()

    @pl.when(has_above)
    def _():
        for z in (0, 1):
            to_above(z).start()

    arrived(buf_z, 1 - hi, z_recv)

    @pl.when(has_above)
    def _():
        for z in (0, 1):
            arrived(buf_above, z, above_recv)

    @pl.when(has_below)
    def _():
        for z in (0, 1):
            arrived(buf_below, z, below_recv)

    @pl.when(jnp.logical_not(has_above))
    def _():
        buf_above[...] = jnp.zeros_like(buf_above)

    @pl.when(jnp.logical_not(has_below))
    def _():
        buf_below[...] = jnp.zeros_like(buf_below)

    sums = total(buf_z)
    sums_h = sums[:, :LANES]
    sums_v = sums[:, LANES : 2 * LANES] + total(buf_below)
    sums_w = total(buf_above) + sums[:, 2 * LANES :]

    site = iota((SITES, 1), 0).astype(F32)
    weight = 1.0 + 2.0 * site / SITES + row.astype(F32) / rows_total
    weight_above = 1.0 + 2.0 * site / SITES + (row - 1).astype(F32) / rows_total
    energy_h, lam_h = finish(sums_h, coupling, jnp.where(site < SITES - 1, weight, 0.0))
    energy_v, lam_v = finish(sums_v, coupling, weight * has_below.astype(F32))
    _, lam_w = finish(sums_w, coupling, weight_above * has_above.astype(F32))
    lam_h, lam_v, lam_w = lam_h.astype(F32), lam_v.astype(F32), lam_w.astype(F32)
    square = squares(sums_h, lam_h) + squares(sums_v, lam_v)
    energies = (energy_h + energy_v).sum()
    lane = iota((SITES, 128), 1)
    message = jnp.where(lane == 0, square, jnp.where(lane == 1, energies, 0.0))
    sends += gather(message, buf_row, row, mates, row_send, row_recv)

    to_right = block(lam_h, 0, 1, False).astype(BF16)
    to_left = block_t(lam_h, 1).astype(BF16)
    to_down = block(lam_v, 0, 0, False).astype(BF16)
    to_up = block_t(lam_w, 0).astype(BF16)

    for i in range(1, rows_total):
        arrived(buf_row, (row + i) % rows_total, row_recv)
    message = total(buf_row)
    square = jnp.maximum(message[:1, :1], 0.0)
    scale = 1.0 / jnp.sqrt(square / (4.0 * rows_total * FLAT * cols_total * cut) + 1e-06)
    energy[...] = message[:1, 1:2] / SITES

    def put(ref, at, value):
        ref[:, :, at] = value.astype(BF16).reshape(PAIRS, SITES, STEP)

    @pl.loop(0, 2 * steps)
    def _(i):
        at = span(i * STEP)
        put(g_right, at, dot16(to_right, signed(v_left, at)) * scale)
        put(g_left, at, dot16(to_left, flat(v_right, at)) * (sign[...] * scale))

    def grad_down(at):
        put(g_down, at, dot16(to_down, signed(from_below, at)) * scale)

    def grad_up(at):
        put(g_up, at, dot16(to_up, flat(from_above, at)) * (sign[...] * scale))

    @pl.loop(0, 2 * steps)
    def _(i):
        at, at_up = span(i * STEP), span(up_start(i))

        @pl.when(has_above)
        def _():
            @pl.when(i >= steps)
            def _():
                send_down(i).wait_recv()

            grad_up(at)

        @pl.when(has_below)
        def _():
            @pl.when(i >= steps)
            def _():
                send_up(i).wait_recv()

            grad_down(at_up)

    @pl.when(jnp.logical_not(has_above))
    def _():
        g_up[...] = jnp.zeros_like(g_up)

    @pl.when(jnp.logical_not(has_below))
    def _():
        g_down[...] = jnp.zeros_like(g_down)

    @pl.when(has_below)
    def _():
        for i in range(steps, 2 * steps):
            send_down(i).wait_send()
        for z in (0, 1):
            to_below(z).wait_send()

    @pl.when(has_above)
    def _():
        for i in range(steps, 2 * steps):
            send_up(i).wait_send()
        for z in (0, 1):
            to_above(z).wait_send()

    for copy in sends:
        copy.wait_send()


def shards(nx, ny, cols_total, right_env, left_env, down_env, up_env, hamiltonian, parity):
    rows_total = lax.axis_size("row")
    cut = right_env.shape[3]
    chunks = cut // STEP
    envs = [e.transpose(0, 2, 1, 3).reshape(PAIRS, SITES, cut) for e in (right_env, left_env, down_env, up_env)]
    env = (PAIRS, SITES, cut)
    dma = pltpu.SemaphoreType.DMA
    hbm_spec = pl.BlockSpec(memory_space=pltpu.HBM)
    vmem_spec = pl.BlockSpec(memory_space=pltpu.VMEM)
    outs = pl.pallas_call(
        functools.partial(kernel, nx, ny, rows_total, cols_total),
        out_shape=[pltpu.VMEM(env, BF16)] * 4 + [jax.ShapeDtypeStruct((1, 1), F32)],
        in_specs=[hbm_spec] * 6,
        out_specs=[vmem_spec] * 5,
        scratch_shapes=[pltpu.VMEM(env, BF16)] * 6
        + [
            pltpu.VMEM((PAIRS, PAIRS), F32),
            pltpu.SMEM((BOND,), jnp.int32),
            pltpu.VMEM((FLAT, STEP), F32),
        ]
        + [pltpu.VMEM((2 * FLAT, 2 * FLAT), F32)] * 3
        + [
            pltpu.VMEM((nx, SITES, 3 * LANES), F32),
            pltpu.VMEM((ny, SITES, 3 * LANES), F32),
            pltpu.VMEM((2, SITES, 3 * LANES), F32),
            pltpu.VMEM((2, SITES, LANES), F32),
            pltpu.VMEM((2, SITES, LANES), F32),
            pltpu.VMEM((rows_total, SITES, 128), F32),
            dma((6,)),
            dma((chunks,)), dma((chunks,)), dma((chunks,)), dma((chunks,)),
            dma((nx,)), dma((nx,)), dma((ny,)), dma((ny,)), dma((2,)), dma((2,)),
            dma((2,)), dma((2,)), dma((2,)), dma((2,)), dma((rows_total,)), dma((rows_total,)),
        ],
        compiler_params=pltpu.CompilerParams(
            collective_id=0, has_side_effects=True, vmem_limit_bytes=40 * 1024 * 1024
        ),
    )(*[pltpu.with_memory_space_constraint(a, pltpu.HBM) for a in (*envs, hamiltonian, parity)])
    grads = [g.reshape(1, PAIRS, SITES, cut).transpose(0, 2, 1, 3) for g in outs[:4]]
    return (*grads, outs[4].reshape(()))


def solution(mesh):
    spec = P("row", None, None, "col")
    side = 4
    return jax.shard_map(
        functools.partial(shards, side, mesh.shape["col"] // (2 * side), mesh.shape["col"]),
        mesh=mesh,
        in_specs=(spec, spec, spec, spec, P(), P()),
        out_specs=(spec, spec, spec, spec, P()),
        check_vma=False,
    )
```

time: 373 us -> 49.5 us (0.13)
  blocking collectives: 270 us -> 0 us
  Pallas kernels: 0 us -> 43 us
  starting transfers between devices: 35.2 us -> 0 us
  waiting for transfers between devices: 18.1 us -> 0 us
  matrix products: 17.2 us -> 0 us
  other arithmetic: 11.3 us -> 0 us
  local copies, waits for them, and re-layouts: 12.9 us -> 4.05 us
  between operations: 7.28 us -> 2.33 us
    psum x2 -> x0, blocking collectives: 270 us -> none  [the longest x1 198 us: shards(): dens_h, dens_v = lax.psum((dens_h, dens_v), 'col')]
    pallas_call x0 -> x1, Pallas kernels: none -> 43 us  [shards(): pl.pallas_call(functools.partial(kernel, nx, ny, rows_total, cols_total),...]
    ppermute x2 -> x0, starting transfers between devices: 35.2 us -> none  [shifted(): lax.ppermute(value, axis, [(source, source + steps) for source in range(i...]
    ppermute x2 -> x0, waiting for transfers between devices: 18.1 us -> none  [shifted(): lax.ppermute(value, axis, [(source, source + steps) for source in range(i...]
    dot_general x6 -> x0, matrix products: 17.2 us -> none  [the longest x2 9.8 us: bond_grads(): jnp.einsum('rcpq,rcqm->rcpm', bond_lam, signed, preferred_element_type=jn...]
    convert_element_type x6 -> x0, other arithmetic: 4.31 us -> none  [the longest x4 4.27 us: shards(): (piece * grad_scale).astype(jnp.bfloat16)]
    reduce_sum x4 -> x0, other arithmetic: 4.17 us -> none  [the longest x2 2.75 us: square_sum(): total = total + jnp.sum(piece * piece)]
    unnamed x36 -> x4, local copies, waits for them, and re-layouts: 7.6 us -> 4.05 us
  transfers between devices with their start and end apart: 2 -> 0, of which waited for: 2 -> 0; matrix products, arithmetic and copies ran while one was open for 5% -> 0% of each run, Pallas kernels for 0% -> 0%
where the time goes in v1:
time: 49.5 us; the launch traced here: 49.4 us
  Pallas kernels  43 us (87%)
  local copies, waits for them, and re-layouts  4.05 us (8%)
  between operations  2.33 us (5%)
    pallas_call x1, Pallas kernels, shards(): pl.pallas_call(functools.partial(kernel, nx, ny, rows_total, cols_total),...  43 us
    unnamed x4, local copies, waits for them, and re-layouts  4.05 us

profile of v1, /device:TPU:1, one launch (start us, length us, event | category | flops | bytes accessed | tf_op | source)
XLA Modules:
  0.0 49.4 jit_solution(5290220072627562593)
XLA Ops:
  0.6 43.0 %shard_map.101 = (bf16[9,8,8192]{2,1,0:T(8,128)(2,1)S(1)}, bf16[9,8,8192]{2,1,0:T(8,128)(2,1)S(1)}, bf16[9,8,8192]{2,1,0:T(8,128)(2,1)S(1)}, bf16[9,8,8192]{2,1,0:T(8,128)(2,1)S(1)}, f32[1,1]{1,0:T(1,128)}) custom-call(bf16[9,8,8192]{2,1,0:T(8,128)(2,1)} %bitcast.29, bf16[9,8,8192]{2,1,0:T(8,128)(2,1)} %bitcast.30, bf16[9,8,8192]{2,1,0:T(8,128)(2,1)} %bitcast.31, ...), custom_call_target="tpu_custom_call" | custom-call | tf_op jit(solution)/shard_map/pallas_call | solution.py:445
  43.6 1.0 %copy.16 = bf16[1,8,9,8192]{3,1,2,0:T(8,128)(2,1)} copy(bf16[1,8,9,8192]{3,1,2,0:T(8,128)(2,1)S(1)} %bitcast.28) | data formatting | bytes 2359296
  44.6 1.0 %copy.17 = bf16[1,8,9,8192]{3,1,2,0:T(8,128)(2,1)} copy(bf16[1,8,9,8192]{3,1,2,0:T(8,128)(2,1)S(1)} %bitcast.27) | data formatting | bytes 2359296
  45.6 1.0 %copy.18 = bf16[1,8,9,8192]{3,1,2,0:T(8,128)(2,1)} copy(bf16[1,8,9,8192]{3,1,2,0:T(8,128)(2,1)S(1)} %bitcast.26) | data formatting | bytes 2359296
  46.7 1.0 %copy.19 = bf16[1,8,9,8192]{3,1,2,0:T(8,128)(2,1)} copy(bf16[1,8,9,8192]{3,1,2,0:T(8,128)(2,1)S(1)} %bitcast.25) | data formatting | bytes 2359296

commit v2 on v1

v2 whole, which is shorter than its diff:
```python
import functools

import jax
import jax.numpy as jnp
from jax import lax
from jax.experimental import pallas as pl
from jax.experimental.pallas import tpu as pltpu
from jax.sharding import PartitionSpec as P

PAIRS = 9
SITES = 8
FLAT = PAIRS * SITES
BOND = 8
LANES = 128
STEP = 1024
WRITES = 4
MESH = pl.DeviceIdType.MESH
HIGHEST = lax.Precision.HIGHEST
F32 = jnp.float32
BF16 = jnp.bfloat16


def iota(shape, dim):
    return lax.broadcasted_iota(jnp.int32, shape, dim)


def dot32(a, b):
    return jnp.dot(a, b, precision=HIGHEST, preferred_element_type=F32)


def dot16(a, b):
    return jnp.dot(a, b, preferred_element_type=F32)


def sign_tile(par):
    shape = (FLAT, 128)
    pair = iota(shape, 0) // SITES
    lane = iota(shape, 1) % (BOND * BOND)
    ket, bra = lane // BOND, lane % BOND
    par_ket = jnp.zeros(shape, jnp.int32)
    par_bra = jnp.zeros(shape, jnp.int32)
    for bond in range(BOND):
        value = par[bond]
        par_ket = jnp.where(ket == bond, value, par_ket)
        par_bra = jnp.where(bra == bond, value, par_bra)
    exponent = jnp.minimum(pair // 3, 1) * par_ket + jnp.minimum(pair % 3, 1) * par_bra
    return (1 - 2 * (exponent % 2)).astype(F32)


def compact(grams, shifts):
    square = (FLAT, FLAT)
    row_site, col_site = iota(square, 0) % SITES, iota(square, 1) % SITES
    rows = jnp.concatenate(
        [jnp.where(col_site == row_site + shift, gram, 0.0) for gram, shift in zip(grams, shifts, strict=True)],
        axis=0,
    )
    spread = (FLAT, LANES)
    source, lane = iota(spread, 0), iota(spread, 1)
    wide = dot32(rows, (lane % PAIRS == source // SITES).astype(F32))
    keep = lane // PAIRS == source // SITES
    out = []
    for i in range(len(grams)):
        part = jnp.where(keep, wide[i * FLAT : (i + 1) * FLAT], 0.0)
        out.append(part.reshape(PAIRS, SITES, LANES).sum(axis=0))
    return out


def rolled(rows, shift):
    shift %= SITES
    if not shift:
        return rows
    return jnp.concatenate([rows[shift:], rows[:shift]], axis=0)


def lane_coupling(ham):
    shape = (PAIRS, PAIRS)
    p, q = iota(shape, 0), iota(shape, 1)

    def charge(state):
        return jnp.minimum(state, 1)

    same = charge(p // 3) + charge(q // 3) == charge(p % 3) + charge(q % 3)
    coupling = jnp.where(same, ham, 0.0)
    shape = (PAIRS, LANES)
    row, lane = iota(shape, 0), iota(shape, 1)
    wide = dot32(coupling, (lane % PAIRS == row).astype(F32))
    return jnp.where(lane // PAIRS == row, wide, 0.0).sum(axis=0, keepdims=True)


def finish(density, coupling, factor):
    entries = PAIRS * PAIRS
    norm = jnp.sqrt((density * density).sum(axis=1, keepdims=True) / entries + 1e-06)
    trace = (coupling * density).sum(axis=1, keepdims=True)
    energy = factor * trace / norm
    lam = factor * (coupling / norm - trace / (entries * norm**3) * density)
    return energy, lam.astype(BF16).astype(F32)


def block(rows, shift, transposed, exact):
    shape = (FLAT, LANES)
    row, lane = iota(shape, 0), iota(shape, 1)
    tall = jnp.concatenate([rolled(rows, -shift) if transposed else rows] * PAIRS, axis=0)
    mine = lane % PAIRS if transposed else lane // PAIRS
    tall = jnp.where(mine == row // SITES, tall, 0.0)
    shape = (LANES, FLAT)
    source, col = iota(shape, 0), iota(shape, 1)
    other = source // PAIRS if transposed else source % PAIRS
    pick = (other == col // SITES).astype(F32)
    wide = dot32(tall, pick) if exact else dot16(tall.astype(BF16), pick.astype(BF16))
    shape = (FLAT, FLAT)
    row_site, col_site = iota(shape, 0) % SITES, iota(shape, 1) % SITES
    hit = row_site == col_site + shift if transposed else col_site == row_site + shift
    return jnp.where(hit, wide, 0.0)


def thirds(value):
    high = value.astype(BF16)
    rest = value - high.astype(F32)
    middle = rest.astype(BF16)
    return high, middle, (rest - middle.astype(F32)).astype(BF16)


def kernel(
    nx, ny, rows_total,
    right, left, down, up, ham_hbm, par_hbm,
    g_right, g_left, g_down, g_up, totals,
    v_right, v_left, v_down, v_up, from_above, from_below, ham, par, sign,
    gram_h, gram_dd, gram_uu, gram_d, gram_u, early_x, early_y, early_z, late_x, late_y, late_z,
    late_above, late_below, buf_row,
    load_sem, down_send, down_recv, up_send, up_recv,
    ex_send, ex_recv, ey_send, ey_recv, ez_send, ez_recv,
    x_send, x_recv, y_send, y_recv, z_send, z_recv,
    above_send, above_recv, below_send, below_recv, row_send, row_recv,
):
    cut = right.shape[2]
    half = cut // 2
    steps = half // STEP
    row, col = lax.axis_index("row"), lax.axis_index("col")
    x, y, hi = col % nx, col // nx % ny, col // (nx * ny)
    plane = nx * ny
    has_above, has_below = row > 0, row < rows_total - 1

    pairs = (
        (ham_hbm, ham), (par_hbm, par), (right, v_right), (left, v_left), (down, v_down), (up, v_up),
    )
    loads = [
        pltpu.make_async_copy(source, target, load_sem.at[i]) for i, (source, target) in enumerate(pairs)
    ]
    for load in loads:
        load.start()

    same_x = [(row, hi * plane + y * nx + (x + i) % nx) for i in range(1, nx)]
    same_y = [(row, hi * plane + (y + i) % ny * nx + x) for i in range(1, ny)]
    partner = (row, (1 - hi) * plane + y * nx + x)
    mates = [((row + i) % rows_total, col) for i in range(1, rows_total)]
    here = y * nx + x
    aboves = [(row - 1, z * plane + here) for z in (0, 1)]
    belows = [(row + 1, z * plane + here) for z in (0, 1)]

    barrier = pltpu.get_barrier_semaphore()
    for device in same_x + same_y + [partner] + mates:
        pl.semaphore_signal(barrier, inc=1, device_id=device, device_id_type=MESH)

    @pl.when(has_above)
    def _():
        pl.semaphore_signal(barrier, inc=1, device_id=(row - 1, partner[1]), device_id_type=MESH)

    @pl.when(has_below)
    def _():
        pl.semaphore_signal(barrier, inc=1, device_id=(row + 1, partner[1]), device_id_type=MESH)

    count = len(same_x) + len(same_y) + 1 + len(mates)
    pl.semaphore_wait(barrier, count + has_above.astype(jnp.int32) + has_below.astype(jnp.int32))

    def span(start):
        return pl.ds(pl.multiple_of(start, STEP), STEP)

    def send_down(i):
        at = span(i * STEP)
        return pltpu.make_async_remote_copy(
            down.at[:, :, at], from_above.at[:, :, at], down_send.at[i], down_recv.at[i],
            device_id=(row + 1, col), device_id_type=MESH,
        )

    def up_start(i):
        return (i * STEP + half) % cut

    def send_up(i):
        at = span(up_start(i))
        return pltpu.make_async_remote_copy(
            up.at[:, :, at], from_below.at[:, :, at], up_send.at[i], up_recv.at[i],
            device_id=(row - 1, col), device_id_type=MESH,
        )

    for i in range(steps):

        @pl.when(has_below)
        def _(i=i):
            send_down(i).start()

        @pl.when(has_above)
        def _(i=i):
            send_up(i).start()

    for load in loads[:2]:
        load.wait()
    tile = sign_tile(par).astype(BF16)
    sign[...] = jnp.concatenate([tile] * (STEP // 128), axis=1)
    coupling = lane_coupling(ham[...])

    def flat(ref, at):
        return ref[:, :, at].reshape(FLAT, STEP)

    def signed(ref, at):
        value = flat(ref, at) * sign[...]
        ref[:, :, at] = value.reshape(PAIRS, SITES, STEP)
        return value

    def product(first, second):
        return lax.dot_general(first, second, (((1,), (1,)), ((), ())), preferred_element_type=F32)

    for gram in (gram_h, gram_dd, gram_uu, gram_d, gram_u):
        gram[...] = jnp.zeros_like(gram)
    for load in loads[2:]:
        load.wait()

    @pl.loop(0, 2 * steps)
    def _(i):
        at = span(i * STEP)
        data = jnp.concatenate([flat(v_right, at), signed(v_left, at)], axis=0)
        gram_h[...] += product(data, data)
        data = flat(v_down, at)
        gram_dd[...] += product(data, data)
        data = signed(v_up, at)
        gram_uu[...] += product(data, data)

    def gather(value, buf, me, devices, send, recv):
        buf[me] = value
        copies = [
            pltpu.make_async_remote_copy(
                buf.at[me], buf.at[me], send.at[i], recv.at[me], device_id=device, device_id_type=MESH
            )
            for i, device in enumerate(devices)
        ]
        for copy in copies:
            copy.start()
        return copies

    def arrived(buf, slot, recv):
        pltpu.make_async_remote_copy(
            buf.at[slot], buf.at[slot], recv.at[slot], recv.at[slot], device_id=(row, col), device_id_type=MESH
        ).wait_recv()

    def all_arrived(buf, me, recv):
        count = buf.shape[0]
        for i in range(1, count):
            arrived(buf, (me + i) % count, recv)
        value = buf[0]
        for i in range(1, count):
            value = value + buf[i]
        return value

    early = compact(
        [gram_h[:FLAT, FLAT:], gram_h[:FLAT, :FLAT], gram_h[FLAT:, FLAT:], gram_dd[...], gram_uu[...]],
        [1, 0, 0, 0, 0],
    )
    early[2] = rolled(early[2], 1)
    sends = gather(jnp.concatenate(early, axis=1), early_x, x, same_x, ex_send, ex_recv)

    def meet(i):
        at, at_up = span(i * STEP), span(up_start(i))

        @pl.when(has_above)
        def _():
            send_down(i).wait_recv()
            gram_u[...] += product(flat(from_above, at), flat(v_up, at))

        @pl.when(has_below)
        def _():
            send_up(i).wait_recv()
            gram_d[...] += product(flat(v_down, at_up), signed(from_below, at_up))
            send_down(i).wait_send()
            send_down(i + steps).start()

        @pl.when(has_above)
        def _():
            send_up(i).wait_send()
            send_up(i + steps).start()

    for i in range(steps // 2):
        meet(i)
    early = all_arrived(early_x, x, ex_recv)
    sends += gather(early, early_y, y, same_y, ey_send, ey_recv)
    for i in range(steps // 2, steps):
        meet(i)

    late = jnp.concatenate(compact([gram_d[...], gram_u[...]], [0, 0]), axis=1)
    sends += gather(late, late_x, x, same_x, x_send, x_recv)
    early = all_arrived(early_y, y, ey_recv)
    sends += gather(early, early_z, hi, [partner], ez_send, ez_recv)
    late = all_arrived(late_x, x, x_recv)
    sends += gather(late, late_y, y, same_y, y_send, y_recv)
    early = all_arrived(early_z, hi, ez_recv)
    density_h, rr, ll, dd, uu = [early[:, i * LANES : (i + 1) * LANES] for i in range(5)]
    rr, ll, dd, uu = [thirds(block(g, 0, False, True)) for g in (rr, ll, dd, uu)]
    site = iota((SITES, 1), 0).astype(F32)
    weight = 1.0 + 2.0 * site / SITES + row.astype(F32) / rows_total
    weight_above = 1.0 + 2.0 * site / SITES + (row - 1).astype(F32) / rows_total
    energy_h, lam_h = finish(density_h, coupling, jnp.where(site < SITES - 1, weight, 0.0))
    weights = block(lam_h, 0, False, False)
    small = weights.astype(BF16)
    total_h = sum(dot16(small, g) for g in ll) + sum(dot16(g, small) for g in rr)
    square_h = (total_h * weights).sum()
    to_right = block(lam_h, 1, False, False).astype(BF16)
    to_left = block(lam_h, 1, True, False).astype(BF16)
    late = all_arrived(late_y, y, y_recv)

    sends += gather(late, late_z, hi, [partner], z_send, z_recv)

    def to_below(z):
        return pltpu.make_async_remote_copy(
            late_z.at[hi, :, pl.ds(0, LANES)], late_above.at[hi],
            below_send.at[z], above_recv.at[hi], device_id=belows[z], device_id_type=MESH,
        )

    def to_above(z):
        return pltpu.make_async_remote_copy(
            late_z.at[hi, :, pl.ds(LANES, LANES)], late_below.at[hi],
            above_send.at[z], below_recv.at[hi], device_id=aboves[z], device_id_type=MESH,
        )

    @pl.when(has_below)
    def _():
        for z in (0, 1):
            to_below(z).start()

    @pl.when(has_above)
    def _():
        for z in (0, 1):
            to_above(z).start()

    def put(ref, at, value):
        ref[:, :, at] = value.reshape(PAIRS, SITES, STEP)

    @pl.loop(0, 2 * steps)
    def _(i):
        at = span(i * STEP)
        put(g_right, at, dot16(to_right, flat(v_left, at)))
        put(g_left, at, dot16(to_left, flat(v_right, at)) * sign[...].astype(F32))

    late = all_arrived(late_z, hi, z_recv)

    @pl.when(has_above)
    def _():
        for z in (0, 1):
            arrived(late_above, z, above_recv)

    @pl.when(has_below)
    def _():
        for z in (0, 1):
            arrived(late_below, z, below_recv)

    @pl.when(jnp.logical_not(has_above))
    def _():
        late_above[...] = jnp.zeros_like(late_above)

    @pl.when(jnp.logical_not(has_below))
    def _():
        late_below[...] = jnp.zeros_like(late_below)

    density_v = late[:, :LANES] + (late_below[0] + late_below[1])
    density_w = (late_above[0] + late_above[1]) + late[:, LANES:]
    energy_v, lam_v = finish(density_v, coupling, weight * has_below.astype(F32))
    _, lam_w = finish(density_w, coupling, weight_above * has_above.astype(F32))
    weights_v, weights_w = block(lam_v, 0, False, False), block(lam_w, 0, False, False)
    to_down, small = weights_v.astype(BF16), weights_w.astype(BF16)
    total_v = sum(dot16(g, to_down) for g in dd)
    total_w = sum(dot16(small, g) for g in uu)
    square = square_h + (total_v * weights_v + total_w * weights_w).sum()
    energies = (energy_h + energy_v).sum()
    lane = iota((SITES, LANES), 1)
    message = jnp.where(lane == 0, square, jnp.where(lane == 1, energies, 0.0))
    sends += gather(message, buf_row, row, mates, row_send, row_recv)
    to_up = block(lam_w, 0, True, False).astype(BF16)

    @pl.loop(0, 2 * steps)
    def _(i):
        at, at_up = span(i * STEP), span(up_start(i))

        @pl.when(has_above)
        def _():
            @pl.when(i >= steps)
            def _():
                send_down(i).wait_recv()

            put(g_up, at, dot16(to_up, flat(from_above, at)) * sign[...].astype(F32))

        @pl.when(has_below)
        def _():
            @pl.when(i >= steps)
            def _():
                send_up(i).wait_recv()
                signed(from_below, at_up)

            put(g_down, at_up, dot16(to_down, flat(from_below, at_up)))

    @pl.when(jnp.logical_not(has_above))
    def _():
        g_up[...] = jnp.zeros_like(g_up)

    @pl.when(jnp.logical_not(has_below))
    def _():
        g_down[...] = jnp.zeros_like(g_down)

    @pl.when(has_below)
    def _():
        for i in range(steps, 2 * steps):
            send_down(i).wait_send()
        for z in (0, 1):
            to_below(z).wait_send()

    @pl.when(has_above)
    def _():
        for i in range(steps, 2 * steps):
            send_up(i).wait_send()
        for z in (0, 1):
            to_above(z).wait_send()

    totals[...] = all_arrived(buf_row, row, row_recv)
    for copy in sends:
        copy.wait_send()


def scale_kernel(
    count, totals, raw_right, raw_left, raw_down, raw_up,
    g_right, g_left, g_down, g_up, energy, o_right, o_left, o_down, o_up, sems,
):
    message = totals[...]
    square = jnp.maximum(message[:1, :1], 0.0)
    scale = 1.0 / jnp.sqrt(square / count + 1e-06)
    energy[...] = message[:1, 1:2] / SITES
    cut = raw_right.shape[2]
    width = cut // WRITES
    arrays = (
        (raw_right, o_right, g_right), (raw_left, o_left, g_left), (raw_down, o_down, g_down), (raw_up, o_up, g_up),
    )
    copies = []
    for a, (raw, out, target) in enumerate(arrays):
        for i in range(WRITES):
            at = pl.ds(i * width, width)

            @pl.loop(0, PAIRS)
            def _(p, raw=raw, out=out, at=at):
                out[p, :, at] = (raw[p, :, at] * scale).astype(BF16)

            copies.append(pltpu.make_async_copy(out.at[:, :, at], target.at[:, :, at], sems.at[a, i]))
            copies[-1].start()
    for copy in copies:
        copy.wait()


def shards(nx, ny, cols_total, right_env, left_env, down_env, up_env, hamiltonian, parity):
    rows_total = lax.axis_size("row")
    cut = right_env.shape[3]
    chunks = cut // STEP
    envs = [e.transpose(0, 2, 1, 3).reshape(PAIRS, SITES, cut) for e in (right_env, left_env, down_env, up_env)]
    env = (PAIRS, SITES, cut)
    dma = pltpu.SemaphoreType.DMA
    hbm_spec = pl.BlockSpec(memory_space=pltpu.HBM)
    vmem_spec = pl.BlockSpec(memory_space=pltpu.VMEM)
    square = pltpu.VMEM((FLAT, FLAT), F32)
    early, late = 5 * LANES, 2 * LANES
    raw = pl.pallas_call(
        functools.partial(kernel, nx, ny, rows_total),
        out_shape=[pltpu.VMEM(env, F32)] * 4 + [pltpu.VMEM((SITES, LANES), F32)],
        in_specs=[hbm_spec] * 6,
        out_specs=[vmem_spec] * 5,
        scratch_shapes=[pltpu.VMEM(env, BF16)] * 6
        + [
            pltpu.VMEM((PAIRS, PAIRS), F32),
            pltpu.SMEM((BOND,), jnp.int32),
            pltpu.VMEM((FLAT, STEP), BF16),
            pltpu.VMEM((2 * FLAT, 2 * FLAT), F32),
            square, square, square, square,
            pltpu.VMEM((nx, SITES, early), F32),
            pltpu.VMEM((ny, SITES, early), F32),
            pltpu.VMEM((2, SITES, early), F32),
            pltpu.VMEM((nx, SITES, late), F32),
            pltpu.VMEM((ny, SITES, late), F32),
            pltpu.VMEM((2, SITES, late), F32),
            pltpu.VMEM((2, SITES, LANES), F32),
            pltpu.VMEM((2, SITES, LANES), F32),
            pltpu.VMEM((rows_total, SITES, LANES), F32),
            dma((6,)),
            dma((chunks,)), dma((chunks,)), dma((chunks,)), dma((chunks,)),
            dma((nx,)), dma((nx,)), dma((ny,)), dma((ny,)), dma((2,)), dma((2,)),
            dma((nx,)), dma((nx,)), dma((ny,)), dma((ny,)), dma((2,)), dma((2,)),
            dma((2,)), dma((2,)), dma((2,)), dma((2,)), dma((rows_total,)), dma((rows_total,)),
        ],
        compiler_params=pltpu.CompilerParams(
            collective_id=0, has_side_effects=True, vmem_limit_bytes=32 * 1024 * 1024
        ),
    )(*[pltpu.with_memory_space_constraint(a, pltpu.HBM) for a in (*envs, hamiltonian, parity)])
    count = 4.0 * rows_total * FLAT * cols_total * cut
    outs = pl.pallas_call(
        functools.partial(scale_kernel, count),
        out_shape=[jax.ShapeDtypeStruct(env, BF16)] * 4 + [jax.ShapeDtypeStruct((1, 1), F32)],
        in_specs=[vmem_spec] * 5,
        out_specs=[hbm_spec] * 4 + [vmem_spec],
        scratch_shapes=[pltpu.VMEM(env, BF16)] * 4 + [dma((4, WRITES))],
        compiler_params=pltpu.CompilerParams(vmem_limit_bytes=16 * 1024 * 1024),
    )(*[pltpu.with_memory_space_constraint(a, pltpu.VMEM) for a in (raw[4], *raw[:4])])
    grads = [g.reshape(1, PAIRS, SITES, cut).transpose(0, 2, 1, 3) for g in outs[:4]]
    return (*grads, outs[4].reshape(()))


def solution(mesh):
    spec = P("row", None, None, "col")
    side = 4
    return jax.shard_map(
        functools.partial(shards, side, mesh.shape["col"] // (2 * side), mesh.shape["col"]),
        mesh=mesh,
        in_specs=(spec, spec, spec, spec, P(), P()),
        out_specs=(spec, spec, spec, spec, P()),
        check_vma=False,
    )
```

time: 49.5 us -> 41.2 us (0.83)
  local copies, waits for them, and re-layouts: 4.05 us -> 0 us
  Pallas kernels: 43 us -> 40.4 us
  between operations: 2.33 us -> 0.64 us
    unnamed x4 -> x0, local copies, waits for them, and re-layouts: 4.05 us -> none
    pallas_call x1 -> x2, Pallas kernels: 43 us -> 40.4 us  [the longest x1 37.2 us: shards(): pl.pallas_call(functools.partial(kernel, nx, ny, rows_total), out_shape=[...]
where the time goes in v2:
time: 41.2 us; the launch traced here: 41.1 us
  Pallas kernels  40.4 us (98%)
  between operations  0.64 us (2%)
    pallas_call x1, Pallas kernels, shards(): pl.pallas_call(functools.partial(kernel, nx, ny, rows_total), out_shape=[...  37.2 us
    pallas_call x1, Pallas kernels, shards(): pl.pallas_call(functools.partial(scale_kernel, count), out_shape=[jax.Sha...  3.24 us

profile of v2, /device:TPU:1, one launch (start us, length us, event | category | flops | bytes accessed | tf_op | source)
XLA Modules:
  0.0 41.1 jit_solution(12133568877292333342)
XLA Ops:
  0.6 37.2 %shard_map.101 = (f32[9,8,8192]{2,1,0:T(8,128)S(1)}, f32[9,8,8192]{2,1,0:T(8,128)S(1)}, f32[9,8,8192]{2,1,0:T(8,128)S(1)}, f32[9,8,8192]{2,1,0:T(8,128)S(1)}, f32[8,128]{1,0:T(8,128)S(1)}) custom-call(bf16[9,8,8192]{2,1,0:T(8,128)(2,1)} %bitcast.25, bf16[9,8,8192]{2,1,0:T(8,128)(2,1)} %bitcast.26, bf16[9,8,8192]{2,1,0:T(8,128)(2,1)} %bitcast.27, ...), custom_call_target="tpu_custom_call" | custom-call | tf_op jit(solution)/shard_map/pallas_call | solution.py:473
  37.8 3.2 %shard_map.102 = (bf16[9,8,8192]{2,1,0:T(8,128)(2,1)}, bf16[9,8,8192]{2,1,0:T(8,128)(2,1)}, bf16[9,8,8192]{2,1,0:T(8,128)(2,1)}, bf16[9,8,8192]{2,1,0:T(8,128)(2,1)}, f32[1,1]{1,0:T(1,128)}) custom-call(f32[8,128]{1,0:T(8,128)S(1)} %get-tuple-element.15.totals, f32[9,8,8192]{2,1,0:T(8,128)S(1)} %get-tuple-element.16.raw_right, ...), custom_call_target="tpu_custom_call" | custom-call | tf_op jit(solution)/shard_map/pallas_call | solution.py:505

commit v3 on v2

--- a/solution.py
+++ b/solution.py
@@ -125,12 +125,12 @@
     right, left, down, up, ham_hbm, par_hbm,
     g_right, g_left, g_down, g_up, totals,
     v_right, v_left, v_down, v_up, from_above, from_below, ham, par, sign,
-    gram_h, gram_dd, gram_uu, gram_d, gram_u, early_x, early_y, early_z, late_x, late_y, late_z,
+    gram_h, gram_dd, gram_uu, gram_d, gram_u, early_x, early_y, early_z, late_xy, late_z,
     late_above, late_below, buf_row,
     load_sem, down_send, down_recv, up_send, up_recv,
     ex_send, ex_recv, ey_send, ey_recv, ez_send, ez_recv,
-    x_send, x_recv, y_send, y_recv, z_send, z_recv,
-    above_send, above_recv, below_send, below_recv, row_send, row_recv,
+    xy_send, xy_recv, z_send, z_recv,
+    above_send, above_recv, below_send, below_recv, row_send, row_recv, relay,
 ):
     cut = right.shape[2]
     half = cut // 2
@@ -138,6 +138,7 @@
     row, col = lax.axis_index("row"), lax.axis_index("col")
     x, y, hi = col % nx, col // nx % ny, col // (nx * ny)
     plane = nx * ny
+    here = y * nx + x
     has_above, has_below = row > 0, row < rows_total - 1
 
     pairs = (
@@ -149,28 +150,26 @@
     for load in loads:
         load.start()
 
-    same_x = [(row, hi * plane + y * nx + (x + i) % nx) for i in range(1, nx)]
-    same_y = [(row, hi * plane + (y + i) % ny * nx + x) for i in range(1, ny)]
-    partner = (row, (1 - hi) * plane + y * nx + x)
-    mates = [((row + i) % rows_total, col) for i in range(1, rows_total)]
-    here = y * nx + x
-    aboves = [(row - 1, z * plane + here) for z in (0, 1)]
-    belows = [(row + 1, z * plane + here) for z in (0, 1)]
+    core, depth = row % 2, rows_total // 2
+    z_count = 2 * depth
+    z = hi * depth + row // 2
+
+    def device(dx=0, dy=0, dz=0, other=False):
+        at_z = (z + dz) % z_count
+        place = (y + dy) % ny * nx + (x + dx) % nx
+        return (at_z % depth * 2 + (1 - core if other else core), at_z // depth * plane + place)
+
+    def signal(semaphore, target):
+        pl.semaphore_signal(semaphore, inc=1, device_id=target, device_id_type=MESH)
 
     barrier = pltpu.get_barrier_semaphore()
-    for device in same_x + same_y + [partner] + mates:
-        pl.semaphore_signal(barrier, inc=1, device_id=device, device_id_type=MESH)
-
-    @pl.when(has_above)
-    def _():
-        pl.semaphore_signal(barrier, inc=1, device_id=(row - 1, partner[1]), device_id_type=MESH)
-
-    @pl.when(has_below)
-    def _():
-        pl.semaphore_signal(barrier, inc=1, device_id=(row + 1, partner[1]), device_id_type=MESH)
-
-    count = len(same_x) + len(same_y) + 1 + len(mates)
-    pl.semaphore_wait(barrier, count + has_above.astype(jnp.int32) + has_below.astype(jnp.int32))
+    near = [device(dx=1), device(dx=-1), device(dy=1), device(dy=-1), device(other=True)]
+    near += [device(dz=step, other=other) for step in (1, -1) for other in (False, True)]
+    for target in near:
+        signal(barrier, target)
+    pl.semaphore_wait(barrier, len(near))
+    for i, target in enumerate((device(dx=-1), device(dy=-1), device(dz=1), device(dz=-1))):
+        signal(relay.at[i], target)
 
     def span(start):
         return pl.ds(pl.multiple_of(start, STEP), STEP)
@@ -265,6 +264,13 @@
         [1, 0, 0, 0, 0],
     )
     early[2] = rolled(early[2], 1)
+    for i in range(4):
+        pl.semaphore_wait(relay.at[i], 1)
+    for i, step in enumerate((2, -2)):
+        signal(relay.at[4 + i], device(dz=step))
+    same_x = [device(dx=i) for i in range(1, nx)]
+    same_y = [device(dy=i) for i in range(1, ny)]
+    same_plane = [device(dx=i % nx, dy=i // nx) for i in range(1, plane)]
     sends = gather(jnp.concatenate(early, axis=1), early_x, x, same_x, ex_send, ex_recv)
 
     def meet(i):
@@ -295,11 +301,38 @@
         meet(i)
 
     late = jnp.concatenate(compact([gram_d[...], gram_u[...]], [0, 0]), axis=1)
-    sends += gather(late, late_x, x, same_x, x_send, x_recv)
     early = all_arrived(early_y, y, ey_recv)
+    sends += gather(late, late_xy, here, same_plane, xy_send, xy_recv)
+    for i in (4, 5):
+        pl.semaphore_wait(relay.at[i], 1)
+    partner = device(dz=depth)
     sends += gather(early, early_z, hi, [partner], ez_send, ez_recv)
-    late = all_arrived(late_x, x, x_recv)
-    sends += gather(late, late_y, y, same_y, y_send, y_recv)
+    late = all_arrived(late_xy, here, xy_recv)
+
+    sends += gather(late, late_z, hi, [partner], z_send, z_recv)
+
+    def to_below(z):
+        return pltpu.make_async_remote_copy(
+            late_z.at[hi, :, pl.ds(0, LANES)], late_above.at[hi],
+            below_send.at[z], above_recv.at[hi], device_id=(row + 1, z * plane + here), device_id_type=MESH,
+        )
+
+    def to_above(z):
+        return pltpu.make_async_remote_copy(
+            late_z.at[hi, :, pl.ds(LANES, LANES)], late_below.at[hi],
+            above_send.at[z], below_recv.at[hi], device_id=(row - 1, z * plane + here), device_id_type=MESH,
+        )
+
+    @pl.when(has_below)
+    def _():
+        for z in (0, 1):
+            to_below(z).start()
+
+    @pl.when(has_above)
+    def _():
+        for z in (0, 1):
+            to_above(z).start()
+
     early = all_arrived(early_z, hi, ez_recv)
     density_h, rr, ll, dd, uu = [early[:, i * LANES : (i + 1) * LANES] for i in range(5)]
     rr, ll, dd, uu = [thirds(block(g, 0, False, True)) for g in (rr, ll, dd, uu)]
@@ -313,31 +346,6 @@
     square_h = (total_h * weights).sum()
     to_right = block(lam_h, 1, False, False).astype(BF16)
     to_left = block(lam_h, 1, True, False).astype(BF16)
-    late = all_arrived(late_y, y, y_recv)
-
-    sends += gather(late, late_z, hi, [partner], z_send, z_recv)
-
-    def to_below(z):
-        return pltpu.make_async_remote_copy(
-            late_z.at[hi, :, pl.ds(0, LANES)], late_above.at[hi],
-            below_send.at[z], above_recv.at[hi], device_id=belows[z], device_id_type=MESH,
-        )
-
-    def to_above(z):
-        return pltpu.make_async_remote_copy(
-            late_z.at[hi, :, pl.ds(LANES, LANES)], late_below.at[hi],
-            above_send.at[z], below_recv.at[hi], device_id=aboves[z], device_id_type=MESH,
-        )
-
-    @pl.when(has_below)
-    def _():
-        for z in (0, 1):
-            to_below(z).start()
-
-    @pl.when(has_above)
-    def _():
-        for z in (0, 1):
-            to_above(z).start()
 
     def put(ref, at, value):
         ref[:, :, at] = value.reshape(PAIRS, SITES, STEP)
@@ -380,6 +388,7 @@
     energies = (energy_h + energy_v).sum()
     lane = iota((SITES, LANES), 1)
     message = jnp.where(lane == 0, square, jnp.where(lane == 1, energies, 0.0))
+    mates = [device(dz=step, other=other) for step in (0, 1, -1, 2) for other in (False, True)][1:]
     sends += gather(message, buf_row, row, mates, row_send, row_recv)
     to_up = block(lam_w, 0, True, False).astype(BF16)
 
@@ -433,18 +442,19 @@
 
 def scale_kernel(
     count, totals, raw_right, raw_left, raw_down, raw_up,
-    g_right, g_left, g_down, g_up, energy, o_right, o_left, o_down, o_up, sems,
+    g_right, g_left, g_down, g_up, energy, o_right, o_left, o_down, o_up, o_energy, sems, energy_sem,
 ):
     message = totals[...]
     square = jnp.maximum(message[:1, :1], 0.0)
     scale = 1.0 / jnp.sqrt(square / count + 1e-06)
-    energy[...] = message[:1, 1:2] / SITES
+    o_energy[...] = message[:1, 1:2] / SITES
+    copies = [pltpu.make_async_copy(o_energy, energy, energy_sem)]
+    copies[0].start()
     cut = raw_right.shape[2]
     width = cut // WRITES
     arrays = (
         (raw_right, o_right, g_right), (raw_left, o_left, g_left), (raw_down, o_down, g_down), (raw_up, o_up, g_up),
     )
-    copies = []
     for a, (raw, out, target) in enumerate(arrays):
         for i in range(WRITES):
             at = pl.ds(i * width, width)
@@ -485,8 +495,7 @@
             pltpu.VMEM((nx, SITES, early), F32),
             pltpu.VMEM((ny, SITES, early), F32),
             pltpu.VMEM((2, SITES, early), F32),
-            pltpu.VMEM((nx, SITES, late), F32),
-            pltpu.VMEM((ny, SITES, late), F32),
+            pltpu.VMEM((nx * ny, SITES, late), F32),
             pltpu.VMEM((2, SITES, late), F32),
             pltpu.VMEM((2, SITES, LANES), F32),
             pltpu.VMEM((2, SITES, LANES), F32),
@@ -494,8 +503,9 @@
             dma((6,)),
             dma((chunks,)), dma((chunks,)), dma((chunks,)), dma((chunks,)),
             dma((nx,)), dma((nx,)), dma((ny,)), dma((ny,)), dma((2,)), dma((2,)),
-            dma((nx,)), dma((nx,)), dma((ny,)), dma((ny,)), dma((2,)), dma((2,)),
+            dma((nx * ny,)), dma((nx * ny,)), dma((2,)), dma((2,)),
             dma((2,)), dma((2,)), dma((2,)), dma((2,)), dma((rows_total,)), dma((rows_total,)),
+            pltpu.SemaphoreType.REGULAR((6,)),
         ],
         compiler_params=pltpu.CompilerParams(
             collective_id=0, has_side_effects=True, vmem_limit_bytes=32 * 1024 * 1024
@@ -506,8 +516,8 @@
         functools.partial(scale_kernel, count),
         out_shape=[jax.ShapeDtypeStruct(env, BF16)] * 4 + [jax.ShapeDtypeStruct((1, 1), F32)],
         in_specs=[vmem_spec] * 5,
-        out_specs=[hbm_spec] * 4 + [vmem_spec],
-        scratch_shapes=[pltpu.VMEM(env, BF16)] * 4 + [dma((4, WRITES))],
+        out_specs=[hbm_spec] * 5,
+        scratch_shapes=[pltpu.VMEM(env, BF16)] * 4 + [pltpu.VMEM((1, 1), F32), dma((4, WRITES)), dma],
         compiler_params=pltpu.CompilerParams(vmem_limit_bytes=16 * 1024 * 1024),
     )(*[pltpu.with_memory_space_constraint(a, pltpu.VMEM) for a in (raw[4], *raw[:4])])
     grads = [g.reshape(1, PAIRS, SITES, cut).transpose(0, 2, 1, 3) for g in outs[:4]]

time: 41.2 us -> 38.1 us (0.925)
  Pallas kernels: 40.4 us -> 37.4 us
    pallas_call x1, Pallas kernels: 37.2 us -> 34.6 us  [shards(): pl.pallas_call(functools.partial(kernel, nx, ny, rows_total), out_shape=[...]
    pallas_call x1, Pallas kernels: 3.24 us -> 2.74 us  [shards(): pl.pallas_call(functools.partial(scale_kernel, count), out_shape=[jax.Sha...]
where the time goes in v3:
time: 38.1 us; the launch traced here: 38 us
  Pallas kernels  37.4 us (98%)
  between operations  0.64 us (2%)
    pallas_call x1, Pallas kernels, shards(): pl.pallas_call(functools.partial(kernel, nx, ny, rows_total), out_shape=[...  34.6 us
    pallas_call x1, Pallas kernels, shards(): pl.pallas_call(functools.partial(scale_kernel, count), out_shape=[jax.Sha...  2.74 us

profile of v3, /device:TPU:1, one launch (start us, length us, event | category | flops | bytes accessed | tf_op | source)
XLA Modules:
  0.0 38.0 jit_solution(11995889314751601090)
XLA Ops:
  0.6 34.6 %shard_map.101 = (f32[9,8,8192]{2,1,0:T(8,128)S(1)}, f32[9,8,8192]{2,1,0:T(8,128)S(1)}, f32[9,8,8192]{2,1,0:T(8,128)S(1)}, f32[9,8,8192]{2,1,0:T(8,128)S(1)}, f32[8,128]{1,0:T(8,128)S(1)}) custom-call(bf16[9,8,8192]{2,1,0:T(8,128)(2,1)} %bitcast.25, bf16[9,8,8192]{2,1,0:T(8,128)(2,1)} %bitcast.26, bf16[9,8,8192]{2,1,0:T(8,128)(2,1)} %bitcast.27, ...), custom_call_target="tpu_custom_call" | custom-call | tf_op jit(solution)/shard_map/pallas_call | solution.py:483
  35.3 2.7 %shard_map.102 = (bf16[9,8,8192]{2,1,0:T(8,128)(2,1)}, bf16[9,8,8192]{2,1,0:T(8,128)(2,1)}, bf16[9,8,8192]{2,1,0:T(8,128)(2,1)}, bf16[9,8,8192]{2,1,0:T(8,128)(2,1)}, f32[1,1]{1,0:T(1,128)}) custom-call(f32[8,128]{1,0:T(8,128)S(1)} %get-tuple-element.15.totals, f32[9,8,8192]{2,1,0:T(8,128)S(1)} %get-tuple-element.16.raw_right, ...), custom_call_target="tpu_custom_call" | custom-call | tf_op jit(solution)/shard_map/pallas_call | solution.py:515

commit v4 on v3

--- a/solution.py
+++ b/solution.py
@@ -13,7 +13,6 @@
 BOND = 8
 LANES = 128
 STEP = 1024
-WRITES = 4
 MESH = pl.DeviceIdType.MESH
 HIGHEST = lax.Precision.HIGHEST
 F32 = jnp.float32
@@ -301,8 +300,8 @@
         meet(i)
 
     late = jnp.concatenate(compact([gram_d[...], gram_u[...]], [0, 0]), axis=1)
+    sends += gather(late, late_xy, here, same_plane, xy_send, xy_recv)
     early = all_arrived(early_y, y, ey_recv)
-    sends += gather(late, late_xy, here, same_plane, xy_send, xy_recv)
     for i in (4, 5):
         pl.semaphore_wait(relay.at[i], 1)
     partner = device(dz=depth)
@@ -450,20 +449,18 @@
     o_energy[...] = message[:1, 1:2] / SITES
     copies = [pltpu.make_async_copy(o_energy, energy, energy_sem)]
     copies[0].start()
-    cut = raw_right.shape[2]
-    width = cut // WRITES
     arrays = (
         (raw_right, o_right, g_right), (raw_left, o_left, g_left), (raw_down, o_down, g_down), (raw_up, o_up, g_up),
     )
     for a, (raw, out, target) in enumerate(arrays):
-        for i in range(WRITES):
-            at = pl.ds(i * width, width)
-
-            @pl.loop(0, PAIRS)
-            def _(p, raw=raw, out=out, at=at):
+        for p in range(PAIRS):
+
+            @pl.loop(0, raw.shape[2] // STEP, unroll=True)
+            def _(i, p=p, raw=raw, out=out):
+                at = pl.ds(pl.multiple_of(i * STEP, STEP), STEP)
                 out[p, :, at] = (raw[p, :, at] * scale).astype(BF16)
 
-            copies.append(pltpu.make_async_copy(out.at[:, :, at], target.at[:, :, at], sems.at[a, i]))
+            copies.append(pltpu.make_async_copy(out.at[p], target.at[p], sems.at[a, p]))
             copies[-1].start()
     for copy in copies:
         copy.wait()
@@ -517,7 +514,7 @@
         out_shape=[jax.ShapeDtypeStruct(env, BF16)] * 4 + [jax.ShapeDtypeStruct((1, 1), F32)],
         in_specs=[vmem_spec] * 5,
         out_specs=[hbm_spec] * 5,
-        scratch_shapes=[pltpu.VMEM(env, BF16)] * 4 + [pltpu.VMEM((1, 1), F32), dma((4, WRITES)), dma],
+        scratch_shapes=[pltpu.VMEM(env, BF16)] * 4 + [pltpu.VMEM((1, 1), F32), dma((4, PAIRS)), dma],
         compiler_params=pltpu.CompilerParams(vmem_limit_bytes=16 * 1024 * 1024),
     )(*[pltpu.with_memory_space_constraint(a, pltpu.VMEM) for a in (raw[4], *raw[:4])])
     grads = [g.reshape(1, PAIRS, SITES, cut).transpose(0, 2, 1, 3) for g in outs[:4]]

time: 38.1 us -> 36.9 us (0.969)
  Pallas kernels: 37.4 us -> 36.2 us
    pallas_call x1, Pallas kernels: 34.6 us -> 33.7 us  [shards(): pl.pallas_call(functools.partial(kernel, nx, ny, rows_total), out_shape=[...]
where the time goes in v4:
time: 36.9 us; the launch traced here: 36.8 us
  Pallas kernels  36.2 us (98%)
  between operations  0.64 us (2%)
    pallas_call x1, Pallas kernels, shards(): pl.pallas_call(functools.partial(kernel, nx, ny, rows_total), out_shape=[...  33.7 us
    pallas_call x1, Pallas kernels, shards(): pl.pallas_call(functools.partial(scale_kernel, count), out_shape=[jax.Sha...  2.54 us

profile of v4, /device:TPU:1, one launch (start us, length us, event | category | flops | bytes accessed | tf_op | source)
XLA Modules:
  0.0 36.8 jit_solution(12662239704738488416)
XLA Ops:
  0.6 33.7 %shard_map.101 = (f32[9,8,8192]{2,1,0:T(8,128)S(1)}, f32[9,8,8192]{2,1,0:T(8,128)S(1)}, f32[9,8,8192]{2,1,0:T(8,128)S(1)}, f32[9,8,8192]{2,1,0:T(8,128)S(1)}, f32[8,128]{1,0:T(8,128)S(1)}) custom-call(bf16[9,8,8192]{2,1,0:T(8,128)(2,1)} %bitcast.25, bf16[9,8,8192]{2,1,0:T(8,128)(2,1)} %bitcast.26, bf16[9,8,8192]{2,1,0:T(8,128)(2,1)} %bitcast.27, ...), custom_call_target="tpu_custom_call" | custom-call | tf_op jit(solution)/shard_map/pallas_call | solution.py:480
  34.3 2.5 %shard_map.102 = (bf16[9,8,8192]{2,1,0:T(8,128)(2,1)}, bf16[9,8,8192]{2,1,0:T(8,128)(2,1)}, bf16[9,8,8192]{2,1,0:T(8,128)(2,1)}, bf16[9,8,8192]{2,1,0:T(8,128)(2,1)}, f32[1,1]{1,0:T(1,128)}) custom-call(f32[8,128]{1,0:T(8,128)S(1)} %get-tuple-element.15.totals, f32[9,8,8192]{2,1,0:T(8,128)S(1)} %get-tuple-element.16.raw_right, ...), custom_call_target="tpu_custom_call" | custom-call | tf_op jit(solution)/shard_map/pallas_call | solution.py:512

commit v5 on v4

--- a/solution.py
+++ b/solution.py
@@ -12,7 +12,7 @@
 FLAT = PAIRS * SITES
 BOND = 8
 LANES = 128
-STEP = 1024
+STEP = 2048
 MESH = pl.DeviceIdType.MESH
 HIGHEST = lax.Precision.HIGHEST
 F32 = jnp.float32
@@ -269,7 +269,9 @@
         signal(relay.at[4 + i], device(dz=step))
     same_x = [device(dx=i) for i in range(1, nx)]
     same_y = [device(dy=i) for i in range(1, ny)]
-    same_plane = [device(dx=i % nx, dy=i // nx) for i in range(1, plane)]
+    offsets = [(i % nx, i // nx) for i in range(1, plane)]
+    offsets.sort(key=lambda d: -min(d[0], nx - d[0]) - min(d[1], ny - d[1]))
+    same_plane = [device(dx=dx, dy=dy) for dx, dy in offsets]
     sends = gather(jnp.concatenate(early, axis=1), early_x, x, same_x, ex_send, ex_recv)
 
     def meet(i):
@@ -349,12 +351,14 @@
     def put(ref, at, value):
         ref[:, :, at] = value.reshape(PAIRS, SITES, STEP)
 
-    @pl.loop(0, 2 * steps)
-    def _(i):
-        at = span(i * STEP)
-        put(g_right, at, dot16(to_right, flat(v_left, at)))
-        put(g_left, at, dot16(to_left, flat(v_right, at)) * sign[...].astype(F32))
-
+    def grads_h(first, last):
+        @pl.loop(first, last)
+        def _(i):
+            at = span(i * STEP)
+            put(g_right, at, dot16(to_right, flat(v_left, at)))
+            put(g_left, at, dot16(to_left, flat(v_right, at)) * sign[...].astype(F32))
+
+    grads_h(0, steps)
     late = all_arrived(late_z, hi, z_recv)
 
     @pl.when(has_above)
@@ -390,6 +394,7 @@
     mates = [device(dz=step, other=other) for step in (0, 1, -1, 2) for other in (False, True)][1:]
     sends += gather(message, buf_row, row, mates, row_send, row_recv)
     to_up = block(lam_w, 0, True, False).astype(BF16)
+    grads_h(steps, 2 * steps)
 
     @pl.loop(0, 2 * steps)
     def _(i):

time: 36.9 us -> 36 us (0.976)
  Pallas kernels: 36.2 us -> 35.3 us
    pallas_call x1, Pallas kernels: 33.7 us -> 32.8 us  [shards(): pl.pallas_call(functools.partial(kernel, nx, ny, rows_total), out_shape=[...]
where the time goes in v5:
time: 36 us
  Pallas kernels  35.3 us (98%)
  between operations  0.64 us (2%)
    pallas_call x1, Pallas kernels, shards(): pl.pallas_call(functools.partial(kernel, nx, ny, rows_total), out_shape=[...  32.8 us
    pallas_call x1, Pallas kernels, shards(): pl.pallas_call(functools.partial(scale_kernel, count), out_shape=[jax.Sha...  2.54 us

profile of v5, /device:TPU:1, one launch (start us, length us, event | category | flops | bytes accessed | tf_op | source)
XLA Modules:
  0.0 36.0 jit_solution(11637052827428271532)
XLA Ops:
  0.6 32.8 %shard_map.101 = (f32[9,8,8192]{2,1,0:T(8,128)S(1)}, f32[9,8,8192]{2,1,0:T(8,128)S(1)}, f32[9,8,8192]{2,1,0:T(8,128)S(1)}, f32[9,8,8192]{2,1,0:T(8,128)S(1)}, f32[8,128]{1,0:T(8,128)S(1)}) custom-call(bf16[9,8,8192]{2,1,0:T(8,128)(2,1)} %bitcast.25, bf16[9,8,8192]{2,1,0:T(8,128)(2,1)} %bitcast.26, bf16[9,8,8192]{2,1,0:T(8,128)(2,1)} %bitcast.27, ...), custom_call_target="tpu_custom_call" | custom-call | tf_op jit(solution)/shard_map/pallas_call | solution.py:485
  33.4 2.5 %shard_map.102 = (bf16[9,8,8192]{2,1,0:T(8,128)(2,1)}, bf16[9,8,8192]{2,1,0:T(8,128)(2,1)}, bf16[9,8,8192]{2,1,0:T(8,128)(2,1)}, bf16[9,8,8192]{2,1,0:T(8,128)(2,1)}, f32[1,1]{1,0:T(1,128)}) custom-call(f32[8,128]{1,0:T(8,128)S(1)} %get-tuple-element.15.totals, f32[9,8,8192]{2,1,0:T(8,128)S(1)} %get-tuple-element.16.raw_right, ...), custom_call_target="tpu_custom_call" | custom-call | tf_op jit(solution)/shard_map/pallas_call | solution.py:517

commit v6 on v5

--- a/solution.py
+++ b/solution.py
@@ -139,6 +139,7 @@
     plane = nx * ny
     here = y * nx + x
     has_above, has_below = row > 0, row < rows_total - 1
+    row_above, row_below = (row - 1) % rows_total, (row + 1) % rows_total
 
     pairs = (
         (ham_hbm, ham), (par_hbm, par), (right, v_right), (left, v_left), (down, v_down), (up, v_up),
@@ -177,7 +178,7 @@
         at = span(i * STEP)
         return pltpu.make_async_remote_copy(
             down.at[:, :, at], from_above.at[:, :, at], down_send.at[i], down_recv.at[i],
-            device_id=(row + 1, col), device_id_type=MESH,
+            device_id=(row_below, col), device_id_type=MESH,
         )
 
     def up_start(i):
@@ -187,7 +188,7 @@
         at = span(up_start(i))
         return pltpu.make_async_remote_copy(
             up.at[:, :, at], from_below.at[:, :, at], up_send.at[i], up_recv.at[i],
-            device_id=(row - 1, col), device_id_type=MESH,
+            device_id=(row_above, col), device_id_type=MESH,
         )
 
     for i in range(steps):
@@ -310,18 +311,18 @@
     sends += gather(early, early_z, hi, [partner], ez_send, ez_recv)
     late = all_arrived(late_xy, here, xy_recv)
 
-    sends += gather(late, late_z, hi, [partner], z_send, z_recv)
+    late_z[hi] = late
 
     def to_below(z):
         return pltpu.make_async_remote_copy(
             late_z.at[hi, :, pl.ds(0, LANES)], late_above.at[hi],
-            below_send.at[z], above_recv.at[hi], device_id=(row + 1, z * plane + here), device_id_type=MESH,
+            below_send.at[z], above_recv.at[hi], device_id=(row_below, z * plane + here), device_id_type=MESH,
         )
 
     def to_above(z):
         return pltpu.make_async_remote_copy(
             late_z.at[hi, :, pl.ds(LANES, LANES)], late_below.at[hi],
-            above_send.at[z], below_recv.at[hi], device_id=(row - 1, z * plane + here), device_id_type=MESH,
+            above_send.at[z], below_recv.at[hi], device_id=(row_above, z * plane + here), device_id_type=MESH,
         )
 
     @pl.when(has_below)
@@ -333,6 +334,13 @@
     def _():
         for z in (0, 1):
             to_above(z).start()
+
+    sends.append(
+        pltpu.make_async_remote_copy(
+            late_z.at[hi], late_z.at[hi], z_send.at[0], z_recv.at[hi], device_id=partner, device_id_type=MESH
+        )
+    )
+    sends[-1].start()
 
     early = all_arrived(early_z, hi, ez_recv)
     density_h, rr, ll, dd, uu = [early[:, i * LANES : (i + 1) * LANES] for i in range(5)]

time: 36 us -> 36 us (level)
  no operation moved by 1% of the time
where the time goes in v6:
time: 36 us; the launch traced here: 35.9 us
  Pallas kernels  35.2 us (98%)
  between operations  0.64 us (2%)
    pallas_call x1, Pallas kernels, shards(): pl.pallas_call(functools.partial(kernel, nx, ny, rows_total), out_shape=[...  32.7 us
    pallas_call x1, Pallas kernels, shards(): pl.pallas_call(functools.partial(scale_kernel, count), out_shape=[jax.Sha...  2.54 us

profile of v6, /device:TPU:1, one launch (start us, length us, event | category | flops | bytes accessed | tf_op | source)
XLA Modules:
  0.0 35.9 jit_solution(15490412700682173461)
XLA Ops:
  0.6 32.7 %shard_map.101 = (f32[9,8,8192]{2,1,0:T(8,128)S(1)}, f32[9,8,8192]{2,1,0:T(8,128)S(1)}, f32[9,8,8192]{2,1,0:T(8,128)S(1)}, f32[9,8,8192]{2,1,0:T(8,128)S(1)}, f32[8,128]{1,0:T(8,128)S(1)}) custom-call(bf16[9,8,8192]{2,1,0:T(8,128)(2,1)} %bitcast.25, bf16[9,8,8192]{2,1,0:T(8,128)(2,1)} %bitcast.26, bf16[9,8,8192]{2,1,0:T(8,128)(2,1)} %bitcast.27, ...), custom_call_target="tpu_custom_call" | custom-call | tf_op jit(solution)/shard_map/pallas_call | solution.py:493
  33.3 2.5 %shard_map.102 = (bf16[9,8,8192]{2,1,0:T(8,128)(2,1)}, bf16[9,8,8192]{2,1,0:T(8,128)(2,1)}, bf16[9,8,8192]{2,1,0:T(8,128)(2,1)}, bf16[9,8,8192]{2,1,0:T(8,128)(2,1)}, f32[1,1]{1,0:T(1,128)}) custom-call(f32[8,128]{1,0:T(8,128)S(1)} %get-tuple-element.15.totals, f32[9,8,8192]{2,1,0:T(8,128)S(1)} %get-tuple-element.16.raw_right, ...), custom_call_target="tpu_custom_call" | custom-call | tf_op jit(solution)/shard_map/pallas_call | solution.py:525
